TPU v7x, 256 devices: a whole 4x4x8 slice. The times are simulated.
256 devices in a mesh: row: 16 (over x, y_hi, core), col: 16 (over y_lo, z).
Axes of the slice: x: 4, y: 4 (y_hi: 2, y_lo: 2; y = y_hi * 2 + y_lo), z: 8, core: 2. Of those that a mesh axis runs over, the one named last changes fastest.
Arguments:
- statistic: float32 [16384, 16384], P('row', 'col'), may hold values from -6 to 6
- gradient: bfloat16 [16384, 4096], P('row', 'col'), may hold values from -0.75 to 0.75
Outputs:
- updated: float32 [16384, 16384], P('row', 'col')
All inputs are finite; a program needn't handle non-finite values.
Results may differ from a plain program's by a relative error of at most 0.0003.
Values may be sent and summed in bfloat16 or wider, within the bound.
A program may use at most 128 MiB of HBM per device.

v0:
```python
import jax
import jax.numpy as jnp
from jax import lax
from jax.sharding import PartitionSpec as P


def local(statistic, gradient):
    column_panel = lax.all_gather(gradient, "row", axis=0, tiled=True)
    partner = lax.all_to_all(column_panel, "col", split_axis=0, concat_axis=1, tiled=True)
    return statistic + lax.dot_general(
        lax.all_gather(gradient, "col", axis=1, tiled=True),
        partner,
        (((1,), (1,)), ((), ())),
        preferred_element_type=jnp.float32,
    )


def solution(mesh):
    in_specs = (P("row", "col"), P("row", "col"))
    out_specs = P("row", "col")
    return jax.shard_map(local, mesh=mesh, in_specs=in_specs, out_specs=out_specs, check_vma=False)
```

profile of v0, /device:TPU:5, one launch (start us, length us, event | category | flops | bytes accessed | tf_op | source)
XLA Modules:
  0.0 403.0 jit_solution(15560671695776487651)
XLA Ops:
  7.4 0.0 all-gather.5.cloned.1.call-start
  7.4 0.7 all-gather.5.cloned.1.call-update
  8.1 82.4 %all-gather.5.cloned.1.call-done = bf16[16384,256]{1,0:T(8,128)(2,1)} async-done(((bf16[1024,256]{1,0:T(8,128)(2,1)}), bf16[16384,256]{1,0:T(8,128)(2,1)}) %all-gather.5.cloned.1.call-update) | async-done | bytes 8388624 | tf_op jit(solution)/shard_map/all_gather | solution.py:8
  90.5 6.9 %all-to-all-start = ((bf16[16,1024,256]{2,1,0:T(8,128)(2,1)}), bf16[16,1024,256]{2,1,0:T(8,128)(2,1)}, u32[]{:S(2)}, u32[]{:S(2)}) async-start(bf16[16,1024,256]{2,1,0:T(8,128)(2,1)} %bitcast.5), calls=%async_computation | async-start | bytes 16777216 | tf_op jit(solution)/shard_map/all_to_all | solution.py:9
  97.4 0.0 all-gather.3.cloned.1.call-start
  97.5 0.5 all-gather.3.cloned.1.call-update
  98.0 229.4 %all-to-all-done = bf16[16,1024,256]{2,1,0:T(8,128)(2,1)} async-done(((bf16[16,1024,256]{2,1,0:T(8,128)(2,1)}), bf16[16,1024,256]{2,1,0:T(8,128)(2,1)}, u32[]{:S(2)}, u32[]{:S(2)}) %all-to-all-start) | async-done | bytes 8388640 | tf_op jit(solution)/shard_map/all_to_all | solution.py:9
  327.4 12.3 %copy.3 = bf16[1024,16,256]{0,2,1:T(8,128)(2,1)} copy(bf16[1024,16,256]{2,0,1:T(8,128)(2,1)} %bitcast.1) | data formatting | bytes 16777216 | tf_op jit(solution)/shard_map/all_to_all | solution.py:9
  339.7 40.2 %all-gather.3.cloned.1.call-done = bf16[1024,4096]{1,0:T(8,128)(2,1)} async-done(((bf16[1024,256]{1,0:T(8,128)(2,1)}), bf16[1024,4096]{1,0:T(8,128)(2,1)}) %all-gather.3.cloned.1.call-update) | async-done | bytes 8388624 | tf_op jit(solution)/shard_map/all_gather | solution.py:11
  379.9 15.6 %convolution_add_fusion = f32[1024,1024]{1,0:T(8,128)} fusion(f32[1024,1024]{1,0:T(8,128)} %param.2, bf16[1024,4096]{1,0:T(8,128)(2,1)} %all-gather.3.cloned.1.call-done, bf16[1024,4096]{0,1:T(8,128)(2,1)} %bitcast.6), kind=kOutput, calls=%fused_computation | convolution fusion | flops 8590983168 | bytes 25165824 | tf_op jit(solution)/shard_map/dot_general | solution.py:10
Async XLA Ops:
  7.4 83.2 %all-gather.5.cloned.1.call-start = ((), (), s32[]{:S(2)}) async-start(), calls=%async_computation.2 | async-start | bytes 8912896 | tf_op jit(solution)/shard_map/all_gather | solution.py:8
  90.5 236.9 %all-to-all-start = ((bf16[16,1024,256]{2,1,0:T(8,128)(2,1)}), bf16[16,1024,256]{2,1,0:T(8,128)(2,1)}, u32[]{:S(2)}, u32[]{:S(2)}) async-start(bf16[16,1024,256]{2,1,0:T(8,128)(2,1)} %bitcast.5), calls=%async_computation | async-start | bytes 16777216 | tf_op jit(solution)/shard_map/all_to_all | solution.py:9
  97.4 282.5 %all-gather.3.cloned.1.call-start = ((), (), s32[]{:S(2)}) async-start(), calls=%async_computation.1 | async-start | bytes 8912896 | tf_op jit(solution)/shard_map/all_gather | solution.py:11
Sparse Core Ops, SparseCore 0:
  10.9 79.6 all-gather.4
Sparse Core Ops, SparseCore 1:
  99.6 280.2 all-gather.2
where the time goes:
time: 408 us; the launch traced here: 403 us
  waiting for transfers between devices  353 us (87%)
  matrix products  15.6 us (4%)
  between operations  14.8 us (4%)
  local copies, waits for them, and re-layouts  12.3 us (3%)
  starting transfers between devices  6.96 us (2%)
    all_to_all x1, waiting for transfers between devices, local(): lax.all_to_all(column_panel, 'col', split_axis=0, concat_axis=1, tiled=True)  229 us
    all_gather x1, waiting for transfers between devices, local(): column_panel = lax.all_gather(gradient, 'row', axis=0, tiled=True)  82.4 us
    all_gather x1, waiting for transfers between devices, local(): lax.all_gather(gradient, 'col', axis=1, tiled=True)  40.2 us
    dot_general x1, matrix products, local(): lax.dot_general(lax.all_gather(gradient, 'col', axis=1, tiled=True), part...  15.6 us
    all_to_all x1, local copies, waits for them, and re-layouts, local(): lax.all_to_all(column_panel, 'col', split_axis=0, concat_axis=1, tiled=True)  12.3 us
  transfers between devices with their start and end apart: 3, of which 3 were waited for; matrix products, arithmetic and copies ran while one was open for 3% of the time, Pallas kernels for 0%

commit v1 on v0

v1 whole, which is shorter than its diff:
```python
import functools

import jax
import jax.numpy as jnp
from jax import lax
from jax.experimental import pallas as pl
from jax.experimental.pallas import tpu as pltpu
from jax.sharding import PartitionSpec as P

MESH = pl.DeviceIdType.MESH
X, Y, Z = 4, 4, 8
TILES = 16
HALF = 512
DEPTH = 256
ROUNDS = 5
STEPS = 3 * ROUNDS
HOP = 2
LAG = 4 * HOP + 3


def device(x, y, z, core):
    return (x * 4 + (y // 2) * 2 + core, (y % 2) * Z + z)


def kernel(stat_ref, grad_ref, out_ref, rows, part, own_sem, stat_sem, rows_sem, part_sem, send_rows, send_twin, send_x, send_cross):
    r, c = lax.axis_index("row"), lax.axis_index("col")
    x, yh, core = r // 4, (r // 2) % 2, r % 2
    yl, z = c // Z, c % Z
    y = 2 * yh + yl
    first, second = core == 0, core == 1

    x_c, yh_c, core_c = c // 4, (c // 2) % 2, c % 2
    rel = (x - x_c + X) % X
    same = yh == yh_c
    root = same & (rel == 0)

    z_up, z_down = (x, y, (z + 1) % Z), (x, y, (z + Z - 1) % Z)
    mate = (x, 2 * yh + 1 - yl, z)
    twin = device(x, y, z, 1 - core)
    x_up, x_down = device((x + 1) % X, y, z, core), device((x + X - 1) % X, y, z, core)
    x_far = device((x + 2) % X, y, z, core)
    y_far = device(x, (y + 2) % Y, z, core)

    own = 2 * c
    load = [pltpu.make_async_copy(grad_ref.at[pl.ds(h * HALF, HALF)], rows.at[core, own + h], own_sem.at[h]) for h in range(2)]
    for copy in load:
        copy.start()
    stat = pltpu.make_async_copy(stat_ref, out_ref, stat_sem)
    stat.start()

    barrier = pltpu.get_barrier_semaphore()

    def greet(others):
        for other in others:
            pl.semaphore_signal(barrier, inc=1, device_id=other, device_id_type=MESH)
        pl.semaphore_wait(barrier, len(others))

    beside = [device(*at, 0) for at in (z_up, z_down, mate)]

    @pl.when(first)
    def _():
        greet([twin, *beside, *[device(*at, 1) for at in (z_up, z_down, mate)]])

    @pl.when(second)
    def _():
        greet([twin, *beside, x_up, x_down, x_far, y_far])

    for copy in load:
        copy.wait()

    def send_row(b, piece, to):
        pltpu.make_async_remote_copy(
            rows.at[b, piece], rows.at[b, piece], send_rows, rows_sem.at[b, piece], device_id=device(*to, 0), device_id_type=MESH
        ).start()

    def send_part(source, piece, to, sem):
        pltpu.make_async_remote_copy(source.at[piece], part.at[piece], sem, part_sem.at[piece], device_id=to, device_id_type=MESH).start()

    def wait_row(b, piece):
        pltpu.make_async_copy(rows.at[b, piece], rows.at[b, piece], rows_sem.at[b, piece]).wait()

    def wait_part(piece):
        pltpu.make_async_copy(part.at[piece], part.at[piece], part_sem.at[piece]).wait()

    def piece_of(far, mates, h):
        return 2 * (((yl + mates) % 2) * Z + (z + far + Z) % Z) + h

    def crosses_at(far, h):
        d = (far + Z) % Z
        return jnp.where(d < 2, 2, jnp.where((d == 3) | (d == 4), 0, 1 + 2 * h))

    def to_twin(b, piece):
        if b == 1:
            pltpu.make_async_remote_copy(
                rows.at[1, piece], rows.at[1, piece], send_twin, rows_sem.at[1, piece], device_id=twin, device_id_type=MESH
            ).start()

        @pl.when(root & (core_c == b))
        def _():
            send_part(rows.at[b], piece, twin, send_twin)

    def both(s, body):
        body(-s, True)

        @pl.when((s >= 1) & (s <= 3))
        def _():
            body(s, False)

    def gather(n):
        s, j = n // 3, n % 3
        h = jnp.where(j == 0, 1, 0)
        mates = jnp.where(j == 2, 1, 0)

        def one(b, far, up):
            piece = piece_of(far, mates, h)
            last_up = (j == 1) | ((j == 0) & (b == 0))

            def act():
                @pl.when((s >= 1) | (j == 2))
                def _():
                    wait_row(b, piece)

                if up:

                    @pl.when((s < 3) | ((s == 3) & last_up))
                    def _():
                        send_row(b, piece, z_up)

                    @pl.when(s == 0)
                    def _():
                        send_row(b, piece, z_down)
                else:

                    @pl.when((s < 3) | jnp.logical_not(last_up))
                    def _():
                        send_row(b, piece, z_down)

                @pl.when(j == 0)
                def _():
                    send_row(b, piece, mate)

                to_twin(b, piece)

            if b == 0:
                act()
            else:
                pl.when((s >= 1) | (j == 2))(act)

        def body(far, up):
            for b in range(2):
                one(b, far, up)

        both(s, body)

        @pl.when(j == 2)
        def _():
            def body(far, up):
                piece = piece_of(far, 1, 1)
                for b in range(2):
                    wait_row(b, piece)
                    to_twin(b, piece)

            both(s, body)

    lag = [jnp.where(same, HOP * (rel if h == 0 else (X - rel) % X), HOP * (1 + jnp.where(rel == 3, 1, rel))) for h in range(2)]

    def forward(far, mates, h):
        piece = piece_of(far, mates, h)
        here = crosses_at(far, h) == rel

        @pl.when(same | here)
        def _():
            wait_part(piece)

            @pl.when(same & (rel != (1 if h else 3)))
            def _():
                send_part(part, piece, x_down if h else x_up, send_x)

            @pl.when(same & here)
            def _():
                send_part(part, piece, y_far, send_cross)

            @pl.when(jnp.logical_not(same))
            def _():
                send_part(part, piece, x_up, send_x)
                send_part(part, piece, x_down, send_x)
                send_part(part, piece, x_far, send_x)

            send_part(part, piece, twin, send_twin)

    def accept(far, mates, h):
        piece = piece_of(far, mates, h)

        @pl.when(jnp.logical_not(same) & (crosses_at(far, h) != rel))
        def _():
            wait_part(piece)
            send_part(part, piece, twin, send_twin)

    def spread(n):
        for act, lags in ((forward, lag), (accept, [4 * HOP, 4 * HOP])):
            for h in range(2):
                m = n - lags[h]
                s, j = m // 3, m % 3

                @pl.when((m >= 0) & (m < STEPS) & (j == 1 - h))
                def _():
                    both(s, lambda far, up: act(far, 0, h))

                @pl.when((m >= 0) & (m < STEPS) & (j == 2))
                def _():
                    both(s, lambda far, up: act(far, 1, h))

    def multiply(far):
        for mates in range(2):
            for h in range(2):
                piece = piece_of(far, mates, h)
                pl.when(first)(functools.partial(wait_part, piece))
                pl.when(second & ((far != 0) | (mates != 0)))(functools.partial(wait_row, 1, piece))

        t0 = (z + far + Z) % Z
        t1 = Z + t0

        def block(i, carry):
            h, b = i // 4, i % 4
            cols = pl.ds(pl.multiple_of(b * DEPTH, DEPTH), DEPTH)
            at = pl.ds(pl.multiple_of(h * HALF, HALF), HALF)
            sub = pl.ds(pl.multiple_of((b % 2) * DEPTH, DEPTH), DEPTH)
            total = None
            for t in (t0, t1):
                term = lax.dot_general(
                    rows[core, 2 * t + h],
                    part[2 * t + b // 2, sub, :],
                    (((1,), (1,)), ((), ())),
                    preferred_element_type=jnp.float32,
                )
                total = term if total is None else total + term
            out_ref[at, cols] += total
            return carry

        lax.fori_loop(0, 8, block, 0)

    @pl.when(first)
    def _():
        send_row(0, own, mate)

    @pl.when(second)
    def _():
        send_row(1, own, mate)
        for h in (1, 0):
            for to in (z_up, z_down):
                send_row(1, own + h, to)
        send_row(1, own + 1, mate)

        @pl.when(root & (core_c == 1))
        def _():
            for h in range(2):
                pltpu.make_async_copy(rows.at[1, own + h], part.at[own + h], part_sem.at[own + h]).start()

    def step(n, carry):
        @pl.when(first & (n < STEPS))
        def _():
            gather(n)

        @pl.when(second)
        def _():
            spread(n)

        m = n - LAG

        @pl.when(m == 0)
        def _():
            stat.wait()

        s, j = m // 3, m % 3

        @pl.when((m >= 0) & (m < STEPS) & ((j == 0) | ((j == 1) & (s >= 1) & (s <= 3))))
        def _():
            multiply(jnp.where(j == 0, s, -s))

        return carry

    lax.fori_loop(0, STEPS + LAG, step, 0)

    def drain(sem, count):
        pltpu.make_async_copy(part.at[pl.ds(0, count)], part.at[pl.ds(0, count)], sem).wait()

    @pl.when(first)
    def _():
        pltpu.make_async_copy(rows.at[:, pl.ds(0, 27)], rows.at[:, pl.ds(0, 27)], send_rows).wait()

        @pl.when(root & (core_c == 0))
        def _():
            pltpu.make_async_copy(rows.at[:, pl.ds(0, 31)], rows.at[:, pl.ds(0, 31)], send_twin).wait()

        @pl.when(root & (core_c == 1))
        def _():
            pltpu.make_async_copy(rows.at[:, pl.ds(0, 30)], rows.at[:, pl.ds(0, 30)], send_twin).wait()

        @pl.when(jnp.logical_not(root))
        def _():
            drain(send_twin, 30)

    @pl.when(second)
    def _():
        drain(send_rows, 6)
        drain(send_twin, 32)

        @pl.when(same)
        def _():
            drain(send_cross, 8)

            @pl.when(rel % 2 == 0)
            def _():
                drain(send_x, 32)

            @pl.when(rel % 2 == 1)
            def _():
                drain(send_x, 16)

        @pl.when(jnp.logical_not(same))
        def _():
            drain(send_x, 24)


def local(statistic, gradient):
    return pl.pallas_call(
        kernel,
        out_shape=jax.ShapeDtypeStruct(statistic.shape, jnp.float32),
        in_specs=[pl.BlockSpec(memory_space=pl.ANY)] * 2,
        out_specs=pl.BlockSpec(memory_space=pltpu.VMEM),
        scratch_shapes=[
            pltpu.VMEM((2, 2 * TILES, HALF, DEPTH), jnp.bfloat16),
            pltpu.VMEM((2 * TILES, HALF, DEPTH), jnp.bfloat16),
            pltpu.SemaphoreType.DMA((2,)),
            pltpu.SemaphoreType.DMA,
            pltpu.SemaphoreType.DMA((2, 2 * TILES)),
            pltpu.SemaphoreType.DMA((2 * TILES,)),
            pltpu.SemaphoreType.DMA,
            pltpu.SemaphoreType.DMA,
            pltpu.SemaphoreType.DMA,
            pltpu.SemaphoreType.DMA,
        ],
        compiler_params=pltpu.CompilerParams(collective_id=0, has_side_effects=True, vmem_limit_bytes=60 << 20),
        cost_estimate=pl.CostEstimate(flops=2 * 1024 * 1024 * 4096, bytes_accessed=9 << 20, transcendentals=0),
        name="shampoo",
    )(statistic, gradient)


def solution(mesh):
    spec = P("row", "col")
    return jax.shard_map(local, mesh=mesh, in_specs=(spec, spec), out_specs=spec, check_vma=False)
```

time: 408 us -> 134 us (0.33)
  the two profiles are of different devices: /device:TPU:5 before, /device:TPU:24 now
where the time goes in v1:
time: 134 us
  Pallas kernels  129 us (96%)
  local copies, waits for them, and re-layouts  4.79 us (4%)
    pallas_call x1, Pallas kernels, local(): pl.pallas_call(kernel, out_shape=jax.ShapeDtypeStruct(statistic.shape, jn...  129 us
    unnamed x1, local copies, waits for them, and re-layouts  4.79 us

profile of v1, /device:TPU:24, one launch (start us, length us, event | category | flops | bytes accessed | tf_op | source)
XLA Modules:
  0.0 134.1 jit_solution(1393701289150498831)
XLA Ops:
  0.0 129.3 %shampoo.1 = f32[1024,1024]{1,0:T(8,128)} custom-call(f32[1024,1024]{1,0:T(8,128)} %stat_ref.1, bf16[1024,256]{1,0:T(8,128)(2,1)} %grad_ref.1), custom_call_target="tpu_custom_call" | custom-call | flops 8589934592 | bytes 9437184 | tf_op jit(solution)/shard_map/shampoo/pallas_call | solution.py:326
  129.3 4.8 %copy.4 = f32[1024,1024]{1,0:T(8,128)} copy(f32[1024,1024]{1,0:T(8,128)} %shampoo.1) | data formatting | bytes 8388608

commit v2 on v1

v2 whole, which is shorter than its diff:
```python
import functools

import jax
import jax.numpy as jnp
from jax import lax
from jax.experimental import pallas as pl
from jax.experimental.pallas import tpu as pltpu
from jax.sharding import PartitionSpec as P

MESH = pl.DeviceIdType.MESH
X, Y, Z = 4, 4, 8
TILES = 16
HALF = 512
DEPTH = 256
ROUNDS = 5
STEPS = 2 * ROUNDS
LAG = 2
HOP = 2
SPLIT = 2
PIECE = HALF // SPLIT
FIRST_AT, SECOND_AT = 11, 6
ORDER = (
    (1, -1, 2, -1, 3, 5, 6, 7, 0, 4),
    (1, 2, -1, 3, -1, 0, 5, 6, 7, 4),
)


def device(x, y, z, core):
    return (x * 4 + (y // 2) * 2 + core, (y % 2) * Z + z)


def kernel(stat_ref, grad_ref, out_ref, rows, part, own_sem, stat_sem, rows_sem, part_sem, send_rows, send_twin, send_x, send_cross):
    r, c = lax.axis_index("row"), lax.axis_index("col")
    x, yh, core = r // 4, (r // 2) % 2, r % 2
    yl, z = c // Z, c % Z
    y = 2 * yh + yl
    first, second = core == 0, core == 1

    x_c, yh_c, core_c = c // 4, (c // 2) % 2, c % 2
    rel = (x - x_c + X) % X
    same = yh == yh_c
    root = same & (rel == 0)

    z_up, z_down = (x, y, (z + 1) % Z), (x, y, (z + Z - 1) % Z)
    mate = (x, 2 * yh + 1 - yl, z)
    twin = device(x, y, z, 1 - core)
    x_up, x_down = device((x + 1) % X, y, z, core), device((x + X - 1) % X, y, z, core)

    x_m = (1 - yl) * 2 + z // 4
    relay = same & (x == x_m)
    z_of = [(x % 2) * 4 + yh * 2 + b for b in range(2)]
    across = [((x + d) % X, 2 * (1 - yh) + 1 - yl, z) for d in (0, 1, X - 1)]

    own = 2 * SPLIT * c
    load = [
        pltpu.make_async_copy(grad_ref.at[pl.ds(u * PIECE, PIECE)], rows.at[core, own + u], own_sem.at[u]) for u in range(2 * SPLIT)
    ]
    for copy in load:
        copy.start()
    stat = pltpu.make_async_copy(stat_ref, out_ref, stat_sem)
    stat.start()

    barrier = pltpu.get_barrier_semaphore()

    def greet(others):
        for other in others:
            pl.semaphore_signal(barrier, inc=1, device_id=other, device_id_type=MESH)
        pl.semaphore_wait(barrier, len(others))

    beside = [device(*at, 0) for at in (z_up, z_down, mate)]

    @pl.when(first)
    def _():
        greet([twin, *beside, *[device(*at, 1) for at in (z_up, z_down, mate, *across)]])

    @pl.when(second)
    def _():
        greet([twin, *beside, x_up, x_down, *[device(*at, k) for at in across for k in range(2)]])

    for copy in load:
        copy.wait()

    def send_row(b, piece, to):
        pltpu.make_async_remote_copy(
            rows.at[b, piece], rows.at[b, piece], send_rows, rows_sem.at[b, piece], device_id=device(*to, 0), device_id_type=MESH
        ).start()

    def send_part(source, piece, to, sem):
        pltpu.make_async_remote_copy(source.at[piece], part.at[piece], sem, part_sem.at[piece], device_id=to, device_id_type=MESH).start()

    def wait_row(b, piece):
        pltpu.make_async_copy(rows.at[b, piece], rows.at[b, piece], rows_sem.at[b, piece]).wait()

    def wait_part(piece):
        pltpu.make_async_copy(part.at[piece], part.at[piece], part_sem.at[piece]).wait()

    def piece_of(far, mates, h):
        return SPLIT * (2 * (((yl + mates) % 2) * Z + (z + far + Z) % Z) + h)

    def aside(far):
        d = (far + Z) % Z
        return (d >= 1) & (d <= 3)

    def pass_on(b, far, piece, h):
        if b == 1:
            pltpu.make_async_remote_copy(
                rows.at[1, piece], rows.at[1, piece], send_twin, rows_sem.at[1, piece], device_id=twin, device_id_type=MESH
            ).start()

        @pl.when(root & (core_c == b))
        def _():
            send_part(rows.at[b], piece, twin, send_twin)

        @pl.when(relay & (core_c == b))
        def _():
            beside_it = aside(far)

            @pl.when(jnp.logical_not(beside_it))
            def _():
                send_part(rows.at[b], piece, device(*across[0], 1), send_cross)

            @pl.when(beside_it & (h == 0))
            def _():
                send_part(rows.at[b], piece, device(*across[1], 1), send_cross)

            @pl.when(beside_it & (h == 1))
            def _():
                send_part(rows.at[b], piece, device(*across[2], 1), send_cross)

    def both(s, body):
        body(-s, True)

        @pl.when((s >= 1) & (s <= 3))
        def _():
            body(s, False)

    def ring(b, s, up, piece, last_up, skip):
        if up:

            @pl.when(((s < 3) | ((s == 3) & last_up)) & jnp.logical_not(skip & ((z + 1) % Z == z_of[b])))
            def _():
                send_row(b, piece, z_up)

            @pl.when((s == 0) & jnp.logical_not(skip & ((z + Z - 1) % Z == z_of[b])))
            def _():
                send_row(b, piece, z_down)
        else:

            @pl.when(((s < 3) | jnp.logical_not(last_up)) & jnp.logical_not(skip & ((z + Z - 1) % Z == z_of[b])))
            def _():
                send_row(b, piece, z_down)

    def exchanged(b, s, j):
        return (s == 0) | jnp.where(j == 0, z != z_of[1 - b], z == z_of[b])

    def gather(n):
        s, j = n // 2, n % 2
        h = 1 - j

        def body(far, up):
            for b in range(2):

                def act(b=b):
                    for u in range(SPLIT):
                        piece = piece_of(far, 0, h) + u

                        @pl.when(s >= 1)
                        def _():
                            wait_row(b, piece)

                        ring(b, s, up, piece, (j == 0) if b == 0 else (j == 1), False)

                        @pl.when(exchanged(b, s, j))
                        def _():
                            send_row(b, piece, mate)

                        pass_on(b, far, piece, h)

                if b == 0:
                    act()
                else:
                    pl.when(s >= 1)(act)

        @pl.when(n < STEPS)
        def _():
            both(s, body)

        def crossed(far, up):
            for b in range(2):

                @pl.when(exchanged(b, s - LAG // 2, j))
                def _():
                    for u in range(SPLIT):
                        piece = piece_of(far, 1, h) + u
                        wait_row(b, piece)
                        pass_on(b, far, piece, h)

        @pl.when(n >= LAG)
        def _():
            both(s - LAG // 2, crossed)

    def deferred(act):
        for b in range(2):

            @pl.when(z == z_of[1 - b])
            def _():
                def one(far, carry):
                    for u in range(SPLIT):
                        act(b, far, u)
                    return carry

                lax.fori_loop(1, Z, one, 0)

    def gather_rest(s):
        def body(far, up):
            for b in range(2):
                for u in range(SPLIT):
                    piece = piece_of(far, 1, 0) + u

                    @pl.when((s >= 1) & (z != z_of[b]))
                    def _():
                        wait_row(b, piece)

                    ring(b, s, up, piece, b == 0, True)

                    if b == 1:

                        @pl.when((s >= 1) & (z != z_of[b]))
                        def _():
                            pass_on(b, far, piece, 0)

        both(s, body)

    lag = [HOP * (jnp.where(same, 0, 1) + (rel if h == 0 else (X - rel) % X)) for h in range(2)]
    other = jnp.logical_not(same)
    early = jnp.where(same, 0, 1)

    def forward(far, mates, h):
        beside_it = other & aside(far)
        entry = jnp.where(beside_it, 1, 0)
        hop = (rel - entry + X) % X if h == 0 else (2 * X - entry - rel) % X

        @pl.when(jnp.logical_not(beside_it & (rel == 0)))
        def _():
            for u in range(SPLIT):
                piece = piece_of(far, mates, h) + u
                wait_part(piece)

                @pl.when(hop < X - 1 - entry)
                def _():
                    send_part(part, piece, x_down if h else x_up, send_x)

                @pl.when(beside_it & (hop == 0))
                def _():
                    send_part(part, piece, x_up if h else x_down, send_x)

                send_part(part, piece, twin, send_twin)

    def accept(far, mates, h):
        @pl.when(other & aside(far) & (rel == 0))
        def _():
            for u in range(SPLIT):
                piece = piece_of(far, mates, h) + u
                wait_part(piece)
                send_part(part, piece, twin, send_twin)

    def spread(n):
        for act, lags in ((forward, lag), (accept, [3 * HOP, 3 * HOP])):
            for h in range(2):
                m = n - lags[h]

                @pl.when((m >= 0) & (m < STEPS) & (m % 2 == 1 - h))
                def _():
                    both(m // 2, lambda far, up: act(far, early, h))

                @pl.when((m >= LAG) & (m < STEPS + LAG) & (m % 2 == 1 - h))
                def _():
                    both((m - LAG) // 2, lambda far, up: act(far, 1 - early, h))

    def multiply(mates, far):
        ends = (far, jnp.where(far == 0, 4, -far))
        for end in ends:
            tile = piece_of(end, mates, 0)

            @pl.when(first)
            def _():
                for u in range(2 * SPLIT):
                    wait_part(tile + u)

            @pl.when(second & ((end != 0) | (mates != 0)))
            def _():
                for u in range(2 * SPLIT):
                    wait_row(1, tile + u)

        def tiles(ref, *lead):
            return jnp.concatenate(
                [ref[*lead, pl.ds(piece_of(end, mates, 0), 2 * SPLIT)].reshape(2 * HALF, DEPTH) for end in ends], axis=1
            )

        out_ref[...] += lax.dot_general(
            tiles(rows, core), tiles(part), (((1,), (1,)), ((), ())), preferred_element_type=jnp.float32
        )

    @pl.when(second)
    def _():
        for u in (*range(SPLIT, 2 * SPLIT), *range(SPLIT)):
            for to in (z_up, z_down, mate):
                send_row(1, own + u, to)

        @pl.when(root & (core_c == 1))
        def _():
            for u in range(2 * SPLIT):
                pltpu.make_async_copy(rows.at[1, own + u], part.at[own + u], part_sem.at[own + u]).start()

        @pl.when(relay & (core_c == 1))
        def _():
            for u in range(2 * SPLIT):
                send_part(rows.at[1], own + u, device(*across[0], 1), send_cross)

    lag_most = jnp.where(other & (rel == 0), 3 * HOP, jnp.maximum(lag[0], lag[1]))
    rest = STEPS + LAG

    def step(n, carry):
        @pl.when(first & (n < rest))
        def _():
            gather(n)

        @pl.when(first & (n == rest))
        def _():
            deferred(lambda b, far, u: send_row(b, piece_of(far, 0, 1) + u, mate))

        @pl.when(first & (n >= rest) & (n < rest + ROUNDS))
        def _():
            gather_rest(n - rest)

        @pl.when(first & (n == rest + ROUNDS - 1))
        def _():
            def late(b, far, u):
                piece = piece_of(far, 1, 1) + u
                wait_row(b, piece)
                if b == 1:
                    pass_on(b, far, piece, 1)

            deferred(late)

        @pl.when(second)
        def _():
            spread(n)

        m = jnp.where(first, n - FIRST_AT, n - lag_most - SECOND_AT)

        @pl.when(m == 0)
        def _():
            stat.wait()

        turn = jnp.where(first, ORDER[0][-1], ORDER[1][-1])
        for i in range(len(ORDER[0])):
            turn = jnp.where(m == i, jnp.where(first, ORDER[0][i], ORDER[1][i]), turn)

        @pl.when((m >= 0) & (m < len(ORDER[0])) & (turn >= 0))
        def _():
            multiply(turn // 4, turn % 4)

        return carry

    lax.fori_loop(0, STEPS + LAG + 4 * HOP + 8, step, 0)

    def drain(sem, count):
        pltpu.make_async_copy(part.at[pl.ds(0, count * SPLIT)], part.at[pl.ds(0, count * SPLIT)], sem).wait()

    @pl.when(first)
    def _():
        place = (z - z_of[0] + Z) % Z
        more, fewer = place <= 1, (place == 2) | (place == Z - 1)
        for those, count in ((more, 29), (fewer, 25), (jnp.logical_not(more | fewer), 27)):

            @pl.when(those)
            def _():
                half = rows.at[:, pl.ds(0, count * SPLIT)]
                pltpu.make_async_copy(half, half, send_rows).wait()

        @pl.when(root & (core_c == 0))
        def _():
            pltpu.make_async_copy(rows.at[:, pl.ds(0, 31 * SPLIT)], rows.at[:, pl.ds(0, 31 * SPLIT)], send_twin).wait()

        @pl.when(root & (core_c == 1))
        def _():
            pltpu.make_async_copy(rows.at[:, pl.ds(0, 30 * SPLIT)], rows.at[:, pl.ds(0, 30 * SPLIT)], send_twin).wait()

        @pl.when(jnp.logical_not(root))
        def _():
            drain(send_twin, 30)

        @pl.when(relay & (core_c == 0))
        def _():
            drain(send_cross, 32)

        @pl.when(relay & (core_c == 1))
        def _():
            drain(send_cross, 30)

    @pl.when(second)
    def _():
        drain(send_rows, 6)
        drain(send_twin, 32)

        @pl.when(relay & (core_c == 1))
        def _():
            drain(send_cross, 2)

        for at, count, beyond in ((0, 32, 20), (1, 16, 22), (2, 32, 32), (3, 16, 22)):

            @pl.when(same & (rel == at))
            def _():
                drain(send_x, count)

            @pl.when(other & (rel == at))
            def _():
                drain(send_x, beyond)


def local(statistic, gradient):
    return pl.pallas_call(
        kernel,
        out_shape=jax.ShapeDtypeStruct(statistic.shape, jnp.float32),
        in_specs=[pl.BlockSpec(memory_space=pltpu.HBM)] * 2,
        out_specs=pl.BlockSpec(memory_space=pltpu.VMEM),
        scratch_shapes=[
            pltpu.VMEM((2, 2 * SPLIT * TILES, PIECE, DEPTH), jnp.bfloat16),
            pltpu.VMEM((2 * SPLIT * TILES, PIECE, DEPTH), jnp.bfloat16),
            pltpu.SemaphoreType.DMA((2 * SPLIT,)),
            pltpu.SemaphoreType.DMA,
            pltpu.SemaphoreType.DMA((2, 2 * SPLIT * TILES)),
            pltpu.SemaphoreType.DMA((2 * SPLIT * TILES,)),
            pltpu.SemaphoreType.DMA,
            pltpu.SemaphoreType.DMA,
            pltpu.SemaphoreType.DMA,
            pltpu.SemaphoreType.DMA,
        ],
        compiler_params=pltpu.CompilerParams(collective_id=0, has_side_effects=True, vmem_limit_bytes=48 << 20),
        cost_estimate=pl.CostEstimate(flops=2 * 1024 * 1024 * 4096, bytes_accessed=9 << 20, transcendentals=0),
        name="shampoo",
    )(statistic, gradient)


def solution(mesh):
    spec = P("row", "col")
    return jax.shard_map(local, mesh=mesh, in_specs=(spec, spec), out_specs=spec, check_vma=False)
```

time: 134 us -> 105 us (0.78)
  the two profiles are of different devices: /device:TPU:24 before, /device:TPU:1 now
where the time goes in v2:
time: 105 us
  Pallas kernels  102 us (97%)
  local copies, waits for them, and re-layouts  3.06 us (3%)
    pallas_call x1, Pallas kernels, local(): pl.pallas_call(kernel, out_shape=jax.ShapeDtypeStruct(statistic.shape, jn...  102 us
    unnamed x3, local copies, waits for them, and re-layouts  3.06 us

profile of v2, /device:TPU:1, one launch (start us, length us, event | category | flops | bytes accessed | tf_op | source)
XLA Modules:
  0.0 105.0 jit_solution(11604013503399566661)
XLA Ops:
  0.0 0.0 copy-start
  0.0 1.0 copy-done
  1.0 101.9 %shampoo.1 = f32[1024,1024]{1,0:T(8,128)S(1)} custom-call(f32[1024,1024]{1,0:T(8,128)} %stat_ref.1, bf16[1024,256]{1,0:T(8,128)(2,1)S(1)} %copy-done), custom_call_target="tpu_custom_call" | custom-call | flops 8589934592 | bytes 9437184 | tf_op jit(solution)/shard_map/shampoo/pallas_call | solution.py:423
  103.0 2.0 %copy.4 = f32[1024,1024]{1,0:T(8,128)} copy(f32[1024,1024]{1,0:T(8,128)S(1)} %shampoo.1) | data formatting | bytes 8388608
Async XLA Ops:
  0.0 1.0 copy-start

commit v3 on v2

--- a/solution.py
+++ b/solution.py
@@ -15,14 +15,26 @@
 ROUNDS = 5
 STEPS = 2 * ROUNDS
 LAG = 2
+ASIDE = (1, 2, 3)
+TWO_WAYS = (4, 5)
 HOP = 2
 SPLIT = 2
 PIECE = HALF // SPLIT
-FIRST_AT, SECOND_AT = 11, 6
+FIRST_AT, SECOND_AT = 11, 5
 ORDER = (
-    (1, -1, 2, -1, 3, 5, 6, 7, 0, 4),
-    (1, 2, -1, 3, -1, 0, 5, 6, 7, 4),
+    (1, 2, 5, 6, 3, 7, 0, 4, -1, -1, -1, -1, -1, -1, -1),
+    (1, 5, 2, 6, 3, 7, 0, 4, -1, -1, -1, -1, -1, -1, -1),
+    (1, -1, 2, -1, 3, -1, 0, 5, 6, 7, 4, -1, -1, -1, -1),
+    (-1, -1, -1, -1, -1, -1, -1, 1, 2, 3, 0, 5, 6, 7, 4),
 )
+
+
+def div(a, b):
+    return lax.div(a, jnp.int32(b))
+
+
+def mod(a, b):
+    return lax.rem(a, jnp.int32(b))
 
 
 def device(x, y, z, core):
@@ -95,11 +107,10 @@
         pltpu.make_async_copy(part.at[piece], part.at[piece], part_sem.at[piece]).wait()
 
     def piece_of(far, mates, h):
-        return SPLIT * (2 * (((yl + mates) % 2) * Z + (z + far + Z) % Z) + h)
+        return SPLIT * (2 * (mod(yl + mates, 2) * Z + mod(z + far + Z, Z)) + h)
 
     def aside(far):
-        d = (far + Z) % Z
-        return (d >= 1) & (d <= 3)
+        return functools.reduce(jnp.logical_or, [(far == d) | (far == d - Z) for d in ASIDE])
 
     def pass_on(b, far, piece, h):
         if b == 1:
@@ -154,7 +165,7 @@
         return (s == 0) | jnp.where(j == 0, z != z_of[1 - b], z == z_of[b])
 
     def gather(n):
-        s, j = n // 2, n % 2
+        s, j = div(n, 2), mod(n, 2)
         h = 1 - j
 
         def body(far, up):
@@ -188,28 +199,31 @@
         def crossed(far, up):
             for b in range(2):
 
-                @pl.when(exchanged(b, s - LAG // 2, j))
+                @pl.when(z == z_of[b])
                 def _():
                     for u in range(SPLIT):
                         piece = piece_of(far, 1, h) + u
                         wait_row(b, piece)
                         pass_on(b, far, piece, h)
 
-        @pl.when(n >= LAG)
+        @pl.when((n >= LAG) & (n < STEPS + LAG))
         def _():
             both(s - LAG // 2, crossed)
 
-    def deferred(act):
-        for b in range(2):
+    def deferred(act, spans):
+        for b, (start, stop) in enumerate(spans):
 
             @pl.when(z == z_of[1 - b])
             def _():
                 def one(far, carry):
-                    for u in range(SPLIT):
-                        act(b, far, u)
+                    @pl.when(far != Z)
+                    def _():
+                        for u in range(SPLIT):
+                            act(b, far, u)
+
                     return carry
 
-                lax.fori_loop(1, Z, one, 0)
+                lax.fori_loop(start, stop, one, 0)
 
     def gather_rest(s):
         def body(far, up):
@@ -217,7 +231,7 @@
                 for u in range(SPLIT):
                     piece = piece_of(far, 1, 0) + u
 
-                    @pl.when((s >= 1) & (z != z_of[b]))
+                    @pl.when(z != z_of[b])
                     def _():
                         wait_row(b, piece)
 
@@ -225,10 +239,24 @@
 
                     if b == 1:
 
-                        @pl.when((s >= 1) & (z != z_of[b]))
+                        @pl.when(z != z_of[b])
                         def _():
                             pass_on(b, far, piece, 0)
 
+                @pl.when((z != z_of[b]) & ((s == 0) | (z != z_of[1 - b])))
+                def _():
+                    for u in range(SPLIT):
+                        piece = piece_of(far, 1, 1) + u
+                        wait_row(b, piece)
+
+                        @pl.when((z_to[b] == z_of[1 - b]) & (s <= 2) & (far != 2 * b - 1))
+                        def _():
+                            send_row(b, piece, z_up if b == 1 else z_down)
+
+                        if b == 1:
+                            pass_on(b, far, piece, 1)
+
+        z_to = ((z + Z - 1) % Z, (z + 1) % Z)
         both(s, body)
 
     lag = [HOP * (jnp.where(same, 0, 1) + (rel if h == 0 else (X - rel) % X)) for h in range(2)]
@@ -238,7 +266,10 @@
     def forward(far, mates, h):
         beside_it = other & aside(far)
         entry = jnp.where(beside_it, 1, 0)
-        hop = (rel - entry + X) % X if h == 0 else (2 * X - entry - rel) % X
+        two_ways = beside_it
+        for d in TWO_WAYS:
+            two_ways |= (far == d) | (far == d - Z)
+        hop = mod(rel - entry + X, X) if h == 0 else mod(2 * X - entry - rel, X)
 
         @pl.when(jnp.logical_not(beside_it & (rel == 0)))
         def _():
@@ -246,11 +277,11 @@
                 piece = piece_of(far, mates, h) + u
                 wait_part(piece)
 
-                @pl.when(hop < X - 1 - entry)
+                @pl.when(hop < jnp.where(two_ways, X - 2, X - 1))
                 def _():
                     send_part(part, piece, x_down if h else x_up, send_x)
 
-                @pl.when(beside_it & (hop == 0))
+                @pl.when(two_ways & (hop == 0))
                 def _():
                     send_part(part, piece, x_up if h else x_down, send_x)
 
@@ -268,14 +299,15 @@
         for act, lags in ((forward, lag), (accept, [3 * HOP, 3 * HOP])):
             for h in range(2):
                 m = n - lags[h]
-
-                @pl.when((m >= 0) & (m < STEPS) & (m % 2 == 1 - h))
-                def _():
-                    both(m // 2, lambda far, up: act(far, early, h))
-
-                @pl.when((m >= LAG) & (m < STEPS + LAG) & (m % 2 == 1 - h))
-                def _():
-                    both((m - LAG) // 2, lambda far, up: act(far, 1 - early, h))
+                parity = mod(m + 64, 2)
+
+                @pl.when((m >= 0) & (m < STEPS) & (parity == 1 - h))
+                def _():
+                    both(div(m, 2), lambda far, up: act(far, early, h))
+
+                @pl.when((m >= LAG) & (m < STEPS + LAG) & (parity == 1 - h))
+                def _():
+                    both(div(m - LAG, 2), lambda far, up: act(far, 1 - early, h))
 
     def multiply(mates, far):
         ends = (far, jnp.where(far == 0, 4, -far))
@@ -318,30 +350,34 @@
                 send_part(rows.at[1], own + u, device(*across[0], 1), send_cross)
 
     lag_most = jnp.where(other & (rel == 0), 3 * HOP, jnp.maximum(lag[0], lag[1]))
-    rest = STEPS + LAG
+    rest = STEPS - 2
 
     def step(n, carry):
-        @pl.when(first & (n < rest))
+        @pl.when(first & (n < STEPS + LAG))
         def _():
             gather(n)
 
-        @pl.when(first & (n == rest))
-        def _():
-            deferred(lambda b, far, u: send_row(b, piece_of(far, 0, 1) + u, mate))
-
         @pl.when(first & (n >= rest) & (n < rest + ROUNDS))
         def _():
             gather_rest(n - rest)
 
-        @pl.when(first & (n == rest + ROUNDS - 1))
-        def _():
-            def late(b, far, u):
-                piece = piece_of(far, 1, 1) + u
-                wait_row(b, piece)
-                if b == 1:
-                    pass_on(b, far, piece, 1)
-
-            deferred(late)
+        @pl.when(first & (n == STEPS))
+        def _():
+            deferred(lambda b, far, u: send_row(b, piece_of(far, 0, 1) + u, mate), ((4, 7), (2, 5)))
+
+        def late(b, far, u):
+            piece = piece_of(far, 1, 1) + u
+            wait_row(b, piece)
+            if b == 1:
+                pass_on(b, far, piece, 1)
+
+        @pl.when(first & (n == STEPS + LAG - 1))
+        def _():
+            deferred(late, ((7, 12), (5, 10)))
+
+        @pl.when(first & (n == STEPS + LAG))
+        def _():
+            deferred(late, ((4, 7), (2, 5)))
 
         @pl.when(second)
         def _():
@@ -353,31 +389,27 @@
         def _():
             stat.wait()
 
-        turn = jnp.where(first, ORDER[0][-1], ORDER[1][-1])
-        for i in range(len(ORDER[0])):
-            turn = jnp.where(m == i, jnp.where(first, ORDER[0][i], ORDER[1][i]), turn)
-
-        @pl.when((m >= 0) & (m < len(ORDER[0])) & (turn >= 0))
-        def _():
-            multiply(turn // 4, turn % 4)
+        turn = jnp.full((), -1, jnp.int32)
+        for i, turns in enumerate(zip(*ORDER)):
+            now = jnp.where(first, turns[0], jnp.where(root, turns[3], jnp.where(z == z_of[0], turns[2], turns[1])))
+            turn = jnp.where(m == i, now, turn)
+
+        @pl.when(turn >= 0)
+        def _():
+            multiply(div(turn, 4), mod(turn, 4))
 
         return carry
 
     lax.fori_loop(0, STEPS + LAG + 4 * HOP + 8, step, 0)
 
     def drain(sem, count):
-        pltpu.make_async_copy(part.at[pl.ds(0, count * SPLIT)], part.at[pl.ds(0, count * SPLIT)], sem).wait()
+        half = rows.at[:, pl.ds(0, count // 2 * SPLIT)]
+        pltpu.make_async_copy(half, half, sem).wait()
 
     @pl.when(first)
     def _():
-        place = (z - z_of[0] + Z) % Z
-        more, fewer = place <= 1, (place == 2) | (place == Z - 1)
-        for those, count in ((more, 29), (fewer, 25), (jnp.logical_not(more | fewer), 27)):
-
-            @pl.when(those)
-            def _():
-                half = rows.at[:, pl.ds(0, count * SPLIT)]
-                pltpu.make_async_copy(half, half, send_rows).wait()
+        half = rows.at[:, pl.ds(0, 27 * SPLIT)]
+        pltpu.make_async_copy(half, half, send_rows).wait()
 
         @pl.when(root & (core_c == 0))
         def _():
@@ -408,7 +440,8 @@
         def _():
             drain(send_cross, 2)
 
-        for at, count, beyond in ((0, 32, 20), (1, 16, 22), (2, 32, 32), (3, 16, 22)):
+        both_ways, aside_all = 4 * len(TWO_WAYS), 4 * len(ASIDE)
+        for at, count, beyond in ((0, 32 + both_ways, 32 + both_ways - aside_all), (1, 16, 16 + aside_all // 2), (2, 32 - both_ways, 32 - both_ways), (3, 16, 16 + aside_all // 2)):
 
             @pl.when(same & (rel == at))
             def _():

time: 105 us -> 96.7 us (0.921)
  the two profiles are of different devices: /device:TPU:1 before, /device:TPU:5 now
where the time goes in v3:
time: 96.7 us; the launch traced here: 96.6 us
  Pallas kernels  93.5 us (97%)
  local copies, waits for them, and re-layouts  3.06 us (3%)
    pallas_call x1, Pallas kernels, local(): pl.pallas_call(kernel, out_shape=jax.ShapeDtypeStruct(statistic.shape, jn...  93.5 us
    unnamed x3, local copies, waits for them, and re-layouts  3.06 us

profile of v3, /device:TPU:5, one launch (start us, length us, event | category | flops | bytes accessed | tf_op | source)
XLA Modules:
  0.0 96.6 jit_solution(1537904437269756557)
XLA Ops:
  0.0 0.0 copy-start
  0.0 1.0 %copy-done = bf16[1024,256]{1,0:T(8,128)(2,1)S(1)} copy-done((bf16[1024,256]{1,0:T(8,128)(2,1)S(1)}, bf16[1024,256]{1,0:T(8,128)(2,1)}, u32[]{:S(2)}) %copy-start) | copy-done | bytes 524312
  1.0 93.5 %shampoo.1 = f32[1024,1024]{1,0:T(8,128)S(1)} custom-call(f32[1024,1024]{1,0:T(8,128)} %stat_ref.1, bf16[1024,256]{1,0:T(8,128)(2,1)S(1)} %copy-done), custom_call_target="tpu_custom_call" | custom-call | flops 8589934592 | bytes 9437184 | tf_op jit(solution)/shard_map/shampoo/pallas_call | solution.py:456
  94.6 2.0 %copy.4 = f32[1024,1024]{1,0:T(8,128)} copy(f32[1024,1024]{1,0:T(8,128)S(1)} %shampoo.1) | data formatting | bytes 8388608
Async XLA Ops:
  0.0 1.0 %copy-start = (bf16[1024,256]{1,0:T(8,128)(2,1)S(1)}, bf16[1024,256]{1,0:T(8,128)(2,1)}, u32[]{:S(2)}) copy-start(bf16[1024,256]{1,0:T(8,128)(2,1)} %grad_ref.1) | copy-start | bytes 1572868

commit v4 on v3

--- a/solution.py
+++ b/solution.py
@@ -15,8 +15,8 @@
 ROUNDS = 5
 STEPS = 2 * ROUNDS
 LAG = 2
-ASIDE = (1, 2, 3)
-TWO_WAYS = (4, 5)
+ASIDE = ((1, 2, 3), (1, 2, 3))
+TWO_WAYS = ((4, 5), (4,))
 HOP = 2
 SPLIT = 2
 PIECE = HALF // SPLIT
@@ -109,8 +109,13 @@
     def piece_of(far, mates, h):
         return SPLIT * (2 * (mod(yl + mates, 2) * Z + mod(z + far + Z, Z)) + h)
 
-    def aside(far):
-        return functools.reduce(jnp.logical_or, [(far == d) | (far == d - Z) for d in ASIDE])
+    def among(far, distances):
+        return functools.reduce(jnp.logical_or, [(far == d) | (far == d - Z) for d in distances], False)
+
+    def aside(far, h):
+        if isinstance(h, int):
+            return among(far, ASIDE[h])
+        return jnp.where(h == 0, among(far, ASIDE[0]), among(far, ASIDE[1]))
 
     def pass_on(b, far, piece, h):
         if b == 1:
@@ -124,7 +129,7 @@
 
         @pl.when(relay & (core_c == b))
         def _():
-            beside_it = aside(far)
+            beside_it = aside(far, h)
 
             @pl.when(jnp.logical_not(beside_it))
             def _():
@@ -264,11 +269,9 @@
     early = jnp.where(same, 0, 1)
 
     def forward(far, mates, h):
-        beside_it = other & aside(far)
+        beside_it = other & aside(far, h)
         entry = jnp.where(beside_it, 1, 0)
-        two_ways = beside_it
-        for d in TWO_WAYS:
-            two_ways |= (far == d) | (far == d - Z)
+        two_ways = beside_it | among(far, TWO_WAYS[h])
         hop = mod(rel - entry + X, X) if h == 0 else mod(2 * X - entry - rel, X)
 
         @pl.when(jnp.logical_not(beside_it & (rel == 0)))
@@ -288,7 +291,7 @@
                 send_part(part, piece, twin, send_twin)
 
     def accept(far, mates, h):
-        @pl.when(other & aside(far) & (rel == 0))
+        @pl.when(other & aside(far, h) & (rel == 0))
         def _():
             for u in range(SPLIT):
                 piece = piece_of(far, mates, h) + u
@@ -440,8 +443,14 @@
         def _():
             drain(send_cross, 2)
 
-        both_ways, aside_all = 4 * len(TWO_WAYS), 4 * len(ASIDE)
-        for at, count, beyond in ((0, 32 + both_ways, 32 + both_ways - aside_all), (1, 16, 16 + aside_all // 2), (2, 32 - both_ways, 32 - both_ways), (3, 16, 16 + aside_all // 2)):
+        both_ways = 2 * sum(map(len, TWO_WAYS))
+        up, down = (2 * len(distances) for distances in ASIDE)
+        for at, count, beyond in (
+            (0, 32 + both_ways, 32 + both_ways - up - down),
+            (1, 16, 16 + up),
+            (2, 32 - both_ways, 32 - both_ways),
+            (3, 16, 16 + down),
+        ):
 
             @pl.when(same & (rel == at))
             def _():

time: 96.7 us -> 91.8 us (0.949)
  Pallas kernels: 93.5 us -> 88.4 us
    pallas_call x1, Pallas kernels: 93.5 us -> 88.4 us  [local(): pl.pallas_call(kernel, out_shape=jax.ShapeDtypeStruct(statistic.shape, jn...]
where the time goes in v4:
time: 91.8 us; the launch traced here: 91.4 us
  Pallas kernels  88.4 us (96%)
  local copies, waits for them, and re-layouts  3.06 us (3%)
    pallas_call x1, Pallas kernels, local(): pl.pallas_call(kernel, out_shape=jax.ShapeDtypeStruct(statistic.shape, jn...  88.4 us
    unnamed x3, local copies, waits for them, and re-layouts  3.06 us

profile of v4, /device:TPU:5, one launch (start us, length us, event | category | flops | bytes accessed | tf_op | source)
XLA Modules:
  0.0 91.4 jit_solution(3380561625177084913)
XLA Ops:
  0.0 0.0 copy-start
  0.0 1.0 %copy-done = bf16[1024,256]{1,0:T(8,128)(2,1)S(1)} copy-done((bf16[1024,256]{1,0:T(8,128)(2,1)S(1)}, bf16[1024,256]{1,0:T(8,128)(2,1)}, u32[]{:S(2)}) %copy-start) | copy-done | bytes 524312
  1.0 88.4 %shampoo.1 = f32[1024,1024]{1,0:T(8,128)S(1)} custom-call(f32[1024,1024]{1,0:T(8,128)} %stat_ref.1, bf16[1024,256]{1,0:T(8,128)(2,1)S(1)} %copy-done), custom_call_target="tpu_custom_call" | custom-call | flops 8589934592 | bytes 9437184 | tf_op jit(solution)/shard_map/shampoo/pallas_call | solution.py:465
  89.4 2.0 %copy.4 = f32[1024,1024]{1,0:T(8,128)} copy(f32[1024,1024]{1,0:T(8,128)S(1)} %shampoo.1) | data formatting | bytes 8388608
Async XLA Ops:
  0.0 1.0 %copy-start = (bf16[1024,256]{1,0:T(8,128)(2,1)S(1)}, bf16[1024,256]{1,0:T(8,128)(2,1)}, u32[]{:S(2)}) copy-start(bf16[1024,256]{1,0:T(8,128)(2,1)} %grad_ref.1) | copy-start | bytes 1572868

commit v5 on v4

--- a/solution.py
+++ b/solution.py
@@ -15,7 +15,7 @@
 ROUNDS = 5
 STEPS = 2 * ROUNDS
 LAG = 2
-ASIDE = ((1, 2, 3), (1, 2, 3))
+ASIDE = ((1, 2, 3), (1, 2, 6))
 TWO_WAYS = ((4, 5), (4,))
 HOP = 2
 SPLIT = 2
@@ -184,13 +184,13 @@
                         def _():
                             wait_row(b, piece)
 
+                        pass_on(b, far, piece, h)
+
                         ring(b, s, up, piece, (j == 0) if b == 0 else (j == 1), False)
 
                         @pl.when(exchanged(b, s, j))
                         def _():
                             send_row(b, piece, mate)
-
-                        pass_on(b, far, piece, h)
 
                 if b == 0:
                     act()

time: 91.8 us -> 91.6 us (level)
  no operation moved by 1% of the time
where the time goes in v5:
time: 91.6 us; the launch traced here: 91 us
  Pallas kernels  87.9 us (96%)
  local copies, waits for them, and re-layouts  3.06 us (3%)
    pallas_call x1, Pallas kernels, local(): pl.pallas_call(kernel, out_shape=jax.ShapeDtypeStruct(statistic.shape, jn...  87.9 us
    unnamed x3, local copies, waits for them, and re-layouts  3.06 us

profile of v5, /device:TPU:5, one launch (start us, length us, event | category | flops | bytes accessed | tf_op | source)
XLA Modules:
  0.0 91.0 jit_solution(15349752720413289700)
XLA Ops:
  0.0 0.0 copy-start
  0.0 1.0 %copy-done = bf16[1024,256]{1,0:T(8,128)(2,1)S(1)} copy-done((bf16[1024,256]{1,0:T(8,128)(2,1)S(1)}, bf16[1024,256]{1,0:T(8,128)(2,1)}, u32[]{:S(2)}) %copy-start) | copy-done | bytes 524312
  1.0 87.9 %shampoo.1 = f32[1024,1024]{1,0:T(8,128)S(1)} custom-call(f32[1024,1024]{1,0:T(8,128)} %stat_ref.1, bf16[1024,256]{1,0:T(8,128)(2,1)S(1)} %copy-done), custom_call_target="tpu_custom_call" | custom-call | flops 8589934592 | bytes 9437184 | tf_op jit(solution)/shard_map/shampoo/pallas_call | solution.py:465
  88.9 2.0 %copy.4 = f32[1024,1024]{1,0:T(8,128)} copy(f32[1024,1024]{1,0:T(8,128)S(1)} %shampoo.1) | data formatting | bytes 8388608
Async XLA Ops:
  0.0 1.0 %copy-start = (bf16[1024,256]{1,0:T(8,128)(2,1)S(1)}, bf16[1024,256]{1,0:T(8,128)(2,1)}, u32[]{:S(2)}) copy-start(bf16[1024,256]{1,0:T(8,128)(2,1)} %grad_ref.1) | copy-start | bytes 1572868
